TPU v7x, 512 devices: a whole 4x4x16 slice. The times are simulated.
512 devices in a mesh: row: 16 (over x, y), col: 32 (over z, core).
Axes of the slice: x: 4, y: 4, z: 16, core: 2. Of those that a mesh axis runs over, the one named last changes fastest.
Arguments:
- block_tiles: bfloat16 [16, 640, 128, 128], P('row', 'col'), may hold values from -0.15811388 to 0.15811388
- block_rows: int32 [16, 640], P('row', 'col'), may hold values from 0 to 15, as said below
- block_cols: int32 [16, 640], P('row', 'col'), may hold values from 0 to 7, as said below
- counts: int32 [16, 32], P('row', 'col'), may hold values from 1 to 20, as said below
- start_basis: bfloat16 [32768, 256], P('col'), may hold values from -6 to 6
Outputs:
- image_out: bfloat16 [32768, 256], P(('row', 'col'))
- basis_out: bfloat16 [32768, 256], P(('col', 'row'))
Inputs may be any that keep to these rules, and one draw needn't show every extreme that they name: `block_rows`: each entry lies in 0 to 15; within the 20 slots of one slab pair no pair of block row and block column repeats. `block_cols`: each entry lies in 0 to 7; see block_rows. `counts`: some slab pair has all 20 slots live in every draw.
All inputs are finite; a program needn't handle non-finite values.
Results may differ from a plain program's by a relative error of at most 0.025.
Values may be sent and summed in bfloat16 or wider, within the bound.
A program may use at most 64 MiB of HBM per device.

v0:
```python
import jax
import jax.numpy as jnp
from jax import lax
from jax.sharding import Mesh
from jax.sharding import PartitionSpec as P

BLOCK = 128
BRD = 16
BCD = 8
NB = 20
COL = ("col_0", "col_1")
ROW = ("row_0", "row_1")
ROW_COL = ("row_0", "row_1", "col_0", "col_1")
COL_ROW = ("col_0", "col_1", "row_0", "row_1")


def cut_along(value, dim, devices):
    lengths = value.shape
    blocks = value.reshape(*lengths[:dim], devices, lengths[dim] // devices, *lengths[dim + 1 :])
    return jnp.moveaxis(blocks, dim, 0)


def summed_on_arrival(value, axis, dim):
    blocks = cut_along(value, dim, lax.axis_size(axis))
    arrived = lax.all_to_all(blocks, axis, split_axis=0, concat_axis=0, tiled=True)
    return arrived.astype(jnp.float32).sum(axis=0)


def sent_to_all(value, axis):
    devices = lax.axis_size(axis)
    return lax.all_to_all(
        jnp.broadcast_to(value[None], (devices, *value.shape)), axis, 0, 0, tiled=True
    )


def laid_out(blocks, dim):
    blocks = jnp.moveaxis(blocks, 0, dim)
    lengths = blocks.shape
    return blocks.reshape(*lengths[:dim], lengths[dim] * lengths[dim + 1], *lengths[dim + 2 :])


def gathered_copies(value, axis, dim):
    blocks = sent_to_all(value, axis)
    return laid_out(blocks, dim)


def one_axis_at_a_time(value, axes):
    for axis in axes:
        value = lax.psum(value, axis)
    return value


def shards(block_tiles, block_rows, block_cols, counts, start_basis):
    tile_stack = block_tiles[0]
    row_ids = block_rows[0]
    col_ids = block_cols[0]
    live_slots = (jnp.arange(NB, dtype=jnp.int32) < counts[0, 0]).astype(jnp.float32)
    row_select = (row_ids[None, :] == jnp.arange(BRD, dtype=jnp.int32)[:, None]).astype(
        jnp.float32
    ) * live_slots[None, :]
    col_select = (col_ids[None, :] == jnp.arange(BCD, dtype=jnp.int32)[:, None]).astype(
        jnp.float32
    ) * live_slots[None, :]
    col_width = lax.axis_size(COL)
    total_cols = BCD * BLOCK * col_width
    pair_select = (
        (row_select[:, None, :] * col_select[None, :, :])
        .reshape(BRD * BCD, NB)
        .astype(jnp.bfloat16)
    )
    dense_slab = jnp.dot(
        pair_select, tile_stack.reshape(NB, BLOCK * BLOCK), preferred_element_type=jnp.float32
    ).astype(jnp.bfloat16)
    dense_slab = (
        dense_slab.reshape(BRD, BCD, BLOCK, BLOCK)
        .transpose(0, 2, 1, 3)
        .reshape(BRD * BLOCK, BCD * BLOCK)
    )
    basis_slab = start_basis
    image_piece = None
    basis_piece = None
    for iteration in range(2):
        partial_value = jnp.dot(dense_slab, basis_slab, preferred_element_type=jnp.float32)
        image_piece = summed_on_arrival(partial_value.astype(jnp.bfloat16), COL, 0).astype(
            jnp.bfloat16
        )
        image_slab = gathered_copies(image_piece, COL, 0)
        reverse_partial = lax.dot_general(
            dense_slab, image_slab, (((0,), (0,)), ((), ())), preferred_element_type=jnp.float32
        )
        reverse_piece = summed_on_arrival(reverse_partial.astype(jnp.bfloat16), ROW, 0)
        squares = one_axis_at_a_time(jnp.sum(reverse_piece * reverse_piece, axis=0), ROW_COL)
        basis_piece = (reverse_piece * lax.rsqrt(squares / total_cols + 1e-06)).astype(jnp.bfloat16)
        if iteration == 0:
            basis_slab = gathered_copies(basis_piece, ROW, 0)
    return (image_piece, basis_piece)


def solution(mesh):
    finer = Mesh(mesh.devices.reshape(4, 4, 16, 2), ("row_0", "row_1", "col_0", "col_1"))
    in_specs = (P(ROW, COL, None, None), P(ROW, COL), P(ROW, COL), P(ROW, COL), P(COL, None))
    out_specs = (P(ROW_COL, None), P(COL_ROW, None))
    return jax.shard_map(
        shards, mesh=finer, in_specs=in_specs, out_specs=out_specs, check_vma=False
    )
```

profile of v0, /device:TPU:1, one launch (start us, length us, event | category | flops | bytes accessed | tf_op | source)
XLA Modules:
  0.0 412.2 jit_solution(11030896881337518923)
XLA Ops:
  1.4 0.7 fusion.29
  2.0 0.7 fusion.28
  2.7 1.2 pad
  4.4 1.2 convolution_convert_fusion
  5.6 1.3 fusion.12
  6.9 0.6 copy-done.1
  7.5 72.3 %all_to_all.35 = bf16[32,64,256]{2,1,0:T(8,128)(2,1)S(1)} all-to-all(bf16[32,64,256]{2,1,0:T(8,128)(2,1)S(1)} %bitcast.54), channel_id=1, replica_groups=mesh['row_0'=4,'row_1'=4,'col_0'=16,'col_1'=2] {'col_0','col_1'}, dimensions={0} | all-to-all | bytes 2097152 | tf_op jit(solution)/shard_map/all_to_all | solution.py:25
  80.1 59.0 %all_to_all.36 = bf16[32,64,256]{2,1,0:T(8,128)(2,1)S(1)} all-to-all(bf16[32,64,256]{2,1,0:T(8,128)(2,1)S(1)} %broadcast_in_dim.6), channel_id=1, replica_groups=mesh['row_0'=4,'row_1'=4,'col_0'=16,'col_1'=2] {'col_0','col_1'}, dimensions={0} | all-to-all | bytes 2097152 | tf_op jit(solution)/shard_map/all_to_all | solution.py:31
  139.1 3.6 fusion.18
  142.6 15.5 %all_to_all.37 = bf16[16,64,256]{2,1,0:T(8,128)(2,1)S(1)} all-to-all(bf16[16,64,256]{2,1,0:T(8,128)(2,1)S(1)} %bitcast.57), channel_id=1, replica_groups=mesh['row_0'=4,'row_1'=4,'col_0'=16,'col_1'=2] {'row_0','row_1'}, dimensions={0} | all-to-all | bytes 1048576 | tf_op jit(solution)/shard_map/all_to_all | solution.py:25
  158.3 7.8 %psum.56 = f32[256]{0:T(256)S(1)} all-reduce(f32[256]{0:T(256)S(1)} %multiply_reduce_fusion.1), channel_id=1, replica_groups=mesh['row_0'=4,'row_1'=4,'col_0'=16,'col_1'=2] {'row_0'}, use_global_device_ids=true, to_apply=%region_3.0 | all-reduce | flops 256 | bytes 2048 | tf_op jit(solution)/shard_map/psum | solution.py:49
  166.1 6.6 %psum.57 = f32[256]{0:T(256)S(1)} all-reduce(f32[256]{0:T(256)S(1)} %psum.56), channel_id=1, replica_groups=mesh['row_0'=4,'row_1'=4,'col_0'=16,'col_1'=2] {'row_1'}, use_global_device_ids=true, to_apply=%region_4.0 | all-reduce | flops 256 | bytes 2048 | tf_op jit(solution)/shard_map/psum | solution.py:49
  172.7 20.0 %psum.58 = f32[256]{0:T(256)S(1)} all-reduce(f32[256]{0:T(256)S(1)} %psum.57), channel_id=1, replica_groups=mesh['row_0'=4,'row_1'=4,'col_0'=16,'col_1'=2] {'col_0'}, use_global_device_ids=true, to_apply=%region_5.0 | all-reduce | flops 256 | bytes 2048 | tf_op jit(solution)/shard_map/psum | solution.py:49
  192.8 15.3 %psum.59 = f32[256]{0:T(256)S(1)} all-reduce(f32[256]{0:T(256)S(1)} %psum.58), channel_id=1, replica_groups=mesh['row_0'=4,'row_1'=4,'col_0'=16,'col_1'=2] {'col_1'}, use_global_device_ids=true, to_apply=%region_6.0 | all-reduce | flops 256 | bytes 2048 | tf_op jit(solution)/shard_map/psum | solution.py:49
  208.1 13.0 %all_to_all.38 = bf16[16,64,256]{2,1,0:T(8,128)(2,1)S(1)} all-to-all(bf16[16,64,256]{2,1,0:T(8,128)(2,1)S(1)} %broadcast_in_dim.7), channel_id=1, replica_groups=mesh['row_0'=4,'row_1'=4,'col_0'=16,'col_1'=2] {'row_0','row_1'}, dimensions={0} | all-to-all | bytes 1048576 | tf_op jit(solution)/shard_map/all_to_all | solution.py:31
  221.1 3.4 fusion.15
  224.6 62.3 %all_to_all.39 = bf16[32,64,256]{2,1,0:T(8,128)(2,1)S(1)} all-to-all(bf16[32,64,256]{2,1,0:T(8,128)(2,1)S(1)} %bitcast.53), channel_id=1, replica_groups=mesh['row_0'=4,'row_1'=4,'col_0'=16,'col_1'=2] {'col_0','col_1'}, dimensions={0} | all-to-all | bytes 2097152 | tf_op jit(solution)/shard_map/all_to_all | solution.py:25
  287.2 59.0 %all_to_all.40 = bf16[32,64,256]{2,1,0:T(8,128)(2,1)S(1)} all-to-all(bf16[32,64,256]{2,1,0:T(8,128)(2,1)S(1)} %broadcast_in_dim.8), channel_id=1, replica_groups=mesh['row_0'=4,'row_1'=4,'col_0'=16,'col_1'=2] {'col_0','col_1'}, dimensions={0} | all-to-all | bytes 2097152 | tf_op jit(solution)/shard_map/all_to_all | solution.py:31
  346.2 3.6 fusion.21
  349.8 12.0 %all_to_all.41 = bf16[16,64,256]{2,1,0:T(8,128)(2,1)S(1)} all-to-all(bf16[16,64,256]{2,1,0:T(8,128)(2,1)S(1)} %bitcast.56), channel_id=1, replica_groups=mesh['row_0'=4,'row_1'=4,'col_0'=16,'col_1'=2] {'row_0','row_1'}, dimensions={0} | all-to-all | bytes 1048576 | tf_op jit(solution)/shard_map/all_to_all | solution.py:25
  361.8 7.8 %psum.60 = f32[256]{0:T(256)S(1)} all-reduce(f32[256]{0:T(256)S(1)} %multiply_reduce_fusion), channel_id=1, replica_groups=mesh['row_0'=4,'row_1'=4,'col_0'=16,'col_1'=2] {'row_0'}, use_global_device_ids=true, to_apply=%region_10.0 | all-reduce | flops 256 | bytes 2048 | tf_op jit(solution)/shard_map/psum | solution.py:49
  369.6 6.6 %psum.61 = f32[256]{0:T(256)S(1)} all-reduce(f32[256]{0:T(256)S(1)} %psum.60), channel_id=1, replica_groups=mesh['row_0'=4,'row_1'=4,'col_0'=16,'col_1'=2] {'row_1'}, use_global_device_ids=true, to_apply=%region_11.0 | all-reduce | flops 256 | bytes 2048 | tf_op jit(solution)/shard_map/psum | solution.py:49
  376.3 20.0 %psum.62 = f32[256]{0:T(256)S(1)} all-reduce(f32[256]{0:T(256)S(1)} %psum.61), channel_id=1, replica_groups=mesh['row_0'=4,'row_1'=4,'col_0'=16,'col_1'=2] {'col_0'}, use_global_device_ids=true, to_apply=%region_12.0 | all-reduce | flops 256 | bytes 2048 | tf_op jit(solution)/shard_map/psum | solution.py:49
  396.3 15.3 %psum.63 = f32[256]{0:T(256)S(1)} all-reduce(f32[256]{0:T(256)S(1)} %psum.62), channel_id=1, replica_groups=mesh['row_0'=4,'row_1'=4,'col_0'=16,'col_1'=2] {'col_1'}, use_global_device_ids=true, to_apply=%region_13.0 | all-reduce | flops 256 | bytes 2048 | tf_op jit(solution)/shard_map/psum | solution.py:49
  (20 shorter events, 2.0 us)
Async XLA Ops:
  0.6 5.0 %copy-start = (bf16[1024,256]{1,0:T(8,128)(2,1)S(1)}, bf16[1024,256]{1,0:T(8,128)(2,1)}, u32[]{:S(2)}) copy-start(bf16[1024,256]{1,0:T(8,128)(2,1)} %param.9) | copy-start | bytes 1572868
  5.6 1.9 copy-start.1
  287.1 62.7 %copy-start.2 = (bf16[64,256]{1,0:T(8,128)(2,1)}, bf16[64,256]{1,0:T(8,128)(2,1)S(1)}, u32[]{:S(2)}) copy-start(bf16[64,256]{1,0:T(8,128)(2,1)S(1)} %reduce_sum.63) | copy-start | bytes 98308
where the time goes:
time: 413 us; the launch traced here: 412 us
  blocking collectives  393 us (95%)
  matrix products  13 us (3%)
    all_to_all x4, blocking collectives, summed_on_arrival(): lax.all_to_all(blocks, axis, split_axis=0, concat_axis=0, tiled=True)  162 us
    all_to_all x3, blocking collectives, sent_to_all(): lax.all_to_all(jnp.broadcast_to(value[None], (devices, *value.shape)), ax...  131 us
    psum x8, blocking collectives, one_axis_at_a_time(): value = lax.psum(value, axis)  99.5 us

commit v1 on v0

v1 whole, which is shorter than its diff:
```python
import functools

import jax
import jax.numpy as jnp
from jax import lax
from jax.experimental import pallas as pl
from jax.experimental.pallas import tpu as pltpu
from jax.sharding import PartitionSpec as P

BLOCK = 128
BRD = 16
BCD = 8
NB = 20
HALF = 128
TOTAL = 32768.0
F32 = jnp.float32
BF16 = jnp.bfloat16


def kernel(
    tab_ref, tabv_ref, tiles_ref, start_ref, image_ref, basis_ref,
    ptab, ptabv, tl_own, tl_in, dense, bas, rs_f, rs_b, yt, acc, zc, r1, s2, r2, zfin, nbuf, ex_i, ex_b,
    pre_send, pre_recv, loc_sem, zs, zr, xs, xr, ns, nr, es, er,
):
    row = lax.axis_index("row")
    col = lax.axis_index("col")
    x, y = row // 4, row % 4
    z, c = col // 2, col % 2
    sg = 1 - 2 * c

    def at(xx, yy, zz, cc):
        return (((xx + 4) % 4) * 4 + (yy + 4) % 4, ((zz + 16) % 16) * 2 + cc)

    def zat(d):
        return at(x, y, z + d, c)

    def remote(src, dst, ssem, rsem, dev):
        return pltpu.make_async_remote_copy(
            src_ref=src, dst_ref=dst, send_sem=ssem, recv_sem=rsem,
            device_id=dev, device_id_type=pl.DeviceIdType.MESH,
        )

    partner = at(x, y, z, 1 - c)

    def norm_peer(stage, k):
        if stage == 0:
            return at(x + k, y, z, c)
        if stage == 1:
            return at(x, y + k, z, c)
        if stage == 2:
            return at(x, y, (z // 4) * 4 + (z + k) % 4, c)
        return at(x, y, z + 4 * k, c)

    barrier = pltpu.get_barrier_semaphore()
    peers = [partner, zat(1), zat(-1)]
    peers += [norm_peer(st, k) for st in range(4) for k in (1, 2, 3)]
    for dev in peers:
        pl.semaphore_signal(barrier, inc=1, device_id=dev, device_id_type=pl.DeviceIdType.MESH)

    own_tiles = pltpu.make_async_copy(tiles_ref.at[0], tl_own.at[pl.ds(0, NB)], loc_sem.at[0])
    own_tiles.start()
    mine = pl.ds(pl.multiple_of(c * HALF, HALF), HALF)
    theirs = pl.ds(pl.multiple_of((1 - c) * HALF, HALF), HALF)
    own_start = pltpu.make_async_copy(start_ref.at[:, :, :, mine], bas.at[0, c], loc_sem.at[1])
    own_start.start()
    zero_tile = jnp.zeros((BLOCK, BLOCK), BF16)
    tl_own[NB] = zero_tile
    tl_in[NB] = zero_tile

    pl.semaphore_wait(barrier, len(peers))
    pre = [
        remote(tabv_ref, ptabv, pre_send.at[0], pre_recv.at[0], partner),
        remote(tiles_ref.at[0], tl_in.at[pl.ds(0, NB)], pre_send.at[1], pre_recv.at[1], partner),
        remote(start_ref.at[:, :, :, theirs], bas.at[0, c], pre_send.at[2], pre_recv.at[2], partner),
    ]
    for copy in pre:
        copy.start()

    def build(which, tl, table):
        def one_row(i, carry):
            for j in range(BCD):
                dense[which, i, :, j * BLOCK : (j + 1) * BLOCK] = tl[table[0, i * BCD + j]]
            return carry

        lax.fori_loop(0, BRD, one_row, 0)

    own_tiles.wait()
    build(c, tl_own, tab_ref)
    incoming = [
        remote(tabv_ref, ptabv, pre_send.at[0], pre_recv.at[0], partner),
        remote(tiles_ref.at[0], tl_in.at[pl.ds(0, NB)], pre_send.at[1], pre_recv.at[1], partner),
        remote(start_ref.at[:, :, :, theirs], bas.at[0, 1 - c], pre_send.at[2], pre_recv.at[2], partner),
    ]
    incoming[0].wait_recv()
    table_in = pltpu.make_async_copy(ptabv, ptab, loc_sem.at[2])
    table_in.start()
    table_in.wait()
    incoming[1].wait_recv()
    build(1 - c, tl_in, ptab)
    incoming[2].wait_recv()
    own_start.wait()
    for copy in pre:
        copy.wait_send()

    def product(it, d):
        d = (d + 32) % 16
        left = bas[it, 0].reshape(1024, HALF)
        right = bas[it, 1].reshape(1024, HALF)
        return jnp.dot(dense[0, d], left, preferred_element_type=F32) + jnp.dot(
            dense[1, d], right, preferred_element_type=F32
        )

    def z_fwd(it, s, src, dst, phase):
        return remote(src, dst, zs.at[it, phase, 0, s], zr.at[it, phase, 0, s], zat(sg))

    def z_bwd(it, s, src, dst, phase):
        return remote(src, dst, zs.at[it, phase, 1, s], zr.at[it, phase, 1, s], zat(-sg))

    def rs_send_f(it, s):
        src = rs_f.at[it, s]
        return z_fwd(it, s, src, rs_f.at[it, s + 1], 0)

    def rs_send_b(it, s):
        src = rs_b.at[it, s]
        return z_bwd(it, s, src, rs_b.at[it, s + 1], 0)

    def ag_send_f(it, s):
        piece = yt.at[it, (z - sg * s + 32) % 16]
        return z_fwd(it, s, piece, piece, 1)

    def ag_send_b(it, s):
        piece = yt.at[it, (z + sg * s + 32) % 16]
        return z_bwd(it, s, piece, piece, 1)

    def ag_recv_f(it, s):
        piece = yt.at[it, (z - sg * (s + 1) + 32) % 16]
        return z_fwd(it, s, piece, piece, 1)

    def ag_recv_b(it, s):
        piece = yt.at[it, (z + sg * (s + 1) + 32) % 16]
        return z_bwd(it, s, piece, piece, 1)

    def ring_dev(axis, d):
        if axis == 0:
            return at(x + d, y, z, c)
        return at(x, y + d, z, c)

    def coord(axis):
        return x if axis == 0 else y

    def xy_copy(it, phase, stage, h, way, msg, axis, src, dst):
        i = (it, phase, stage, h, way * 3 + msg)
        return remote(src, dst, xs.at[i], xr.at[i], ring_dev(axis, sg if way == 0 else -sg))

    def rs4_copies(it, stage, h, axis):
        buf = zc.at[it, h] if stage == 0 else s2.at[it, h]
        rb = r1.at[it, h] if stage == 0 else r2.at[it, h]
        a = coord(axis)
        far = (a + 2) % 4
        nxt = (a + sg + 4) % 4
        prv = (a - sg + 4) % 4
        plan = [(0, 0, far, 0), (1, 0, far, 1), (0, 1, nxt, 1), (1, 1, prv, 0), (0, 2, nxt, 0), (1, 2, prv, 1)]
        return {
            (way, msg): xy_copy(it, 0, stage, h, way, msg, axis, buf.at[g, sub], rb.at[way * 3 + msg])
            for way, msg, g, sub in plan
        }

    def rs4(it, stage, axes):
        copies = [rs4_copies(it, stage, h, axes[h]) for h in (0, 1)]
        for key in ((0, 0), (1, 0), (0, 1), (1, 1)):
            for h in (0, 1):
                copies[h][key].start()
        for way in (0, 1):
            for h in (0, 1):
                buf, rb = (zc, r1) if stage == 0 else (s2, r2)
                a = coord(axes[h])
                g = (a + sg + 4) % 4 if way == 0 else (a - sg + 4) % 4
                copies[h][way, 0].wait_recv()
                total = buf[it, h, g, way].astype(F32) + rb[it, h, way * 3].astype(F32)
                buf[it, h, g, way] = total.astype(BF16)
                copies[h][way, 2].start()
        result = []
        for h in (0, 1):
            buf, rb = (zc, r1) if stage == 0 else (s2, r2)
            a = coord(axes[h])
            for key in ((0, 1), (1, 1), (0, 2), (1, 2)):
                copies[h][key].wait_recv()
            low = buf[it, h, a, 0].astype(F32) + rb[it, h, 2].astype(F32) + rb[it, h, 4].astype(F32)
            high = buf[it, h, a, 1].astype(F32) + rb[it, h, 1].astype(F32) + rb[it, h, 5].astype(F32)
            result.append((low, high))
        return result, copies

    def piece_ref(it, h, stage, axis, g, sub):
        if stage == 0:
            rows = pl.ds(sub * 32, 32)
            if axis == 0:
                return bas.at[it, h, g, y, rows]
            return bas.at[it, h, x, g, rows]
        pair = pl.ds(sub * 2, 2)
        if axis == 0:
            return bas.at[it, h, g, pair]
        return bas.at[it, h, pair, g]

    def ag4_copies(it, stage, h, axis):
        a = coord(axis)
        nxt = (a + sg + 4) % 4
        prv = (a - sg + 4) % 4
        plan = [(0, 0, a, 0), (1, 0, a, 1), (0, 1, a, 1), (1, 1, a, 0), (0, 2, prv, 0), (1, 2, nxt, 1)]
        out = {}
        for way, msg, g, sub in plan:
            ref = piece_ref(it, h, stage, axis, g, sub)
            out[way, msg] = xy_copy(it, 1, stage, h, way, msg, axis, ref, ref)
        return out

    def ag4_recv(it, stage, h, axis, way, msg):
        a = coord(axis)
        nxt = (a + sg + 4) % 4
        prv = (a - sg + 4) % 4
        far = (a + 2) % 4
        g, sub = {
            (0, 0): (prv, 0), (1, 0): (nxt, 1), (0, 1): (prv, 1),
            (1, 1): (nxt, 0), (0, 2): (far, 0), (1, 2): (far, 1),
        }[way, msg]
        ref = piece_ref(it, h, stage, axis, g, sub)
        xy_copy(it, 1, stage, h, way, msg, axis, ref, ref).wait_recv()

    def ag4_start(it, stage, axes):
        copies = [ag4_copies(it, stage, h, axes[h]) for h in (0, 1)]
        for key in ((0, 0), (1, 0), (0, 1), (1, 1)):
            for h in (0, 1):
                copies[h][key].start()
        return copies

    def ag4_finish(it, stage, axes, copies):
        for way in (0, 1):
            for h in (0, 1):
                ag4_recv(it, stage, h, axes[h], way, 0)
                copies[h][way, 2].start()
        for key in ((0, 1), (1, 1), (0, 2), (1, 2)):
            for h in (0, 1):
                ag4_recv(it, stage, h, axes[h], *key)

    def norm_copy(it, stage, k):
        return remote(
            nbuf.at[it, stage, 0], nbuf.at[it, stage, k], ns.at[it, stage, k], nr.at[it, stage, k],
            norm_peer(stage, k),
        )

    def norm_start(it, stage, value):
        nbuf[it, stage, 0] = jnp.broadcast_to(value, (8, HALF))
        for k in (1, 2, 3):
            norm_copy(it, stage, k).start()

    def norm_finish(it, stage):
        for k in (1, 2, 3):
            norm_copy(it, stage, k).wait_recv()
        return (nbuf[it, stage, 0] + nbuf[it, stage, 1] + nbuf[it, stage, 2] + nbuf[it, stage, 3])[0:1]

    def scale_of(total):
        return lax.rsqrt(total / TOTAL + 1e-06)

    def add_products(it, pieces, first):
        for which in (0, 1):
            for part in range(2):
                cols = pl.ds(part * 512, 512)
                total = None if first else acc[which, :, cols]
                for p in pieces:
                    term = jnp.dot(yt[it, p], dense[which, p, :, cols], preferred_element_type=F32)
                    total = term if total is None else total + term
                acc[which, :, cols] = total

    lane = lax.broadcasted_iota(jnp.int32, (HALF, BLOCK), 1) < 64

    for it in (0, 1):
        rs_f[it, 0] = product(it, z + sg * 8).astype(BF16)
        rs_send_f(it, 0).start()
        rs_b[it, 0] = product(it, z - sg * 7).astype(BF16)
        rs_send_b(it, 0).start()
        if it == 1:
            norm_start(0, 2, norm_finish(0, 1))

        def rs_step(s, carry):
            ahead = product(it, z + sg * (8 - s))
            behind = product(it, z - sg * (7 - s))
            rs_send_f(it, s - 1).wait_recv()
            rs_f[it, s] = (ahead + rs_f[it, s].astype(F32)).astype(BF16)
            rs_send_f(it, s).start()
            rs_send_b(it, s - 1).wait_recv()
            rs_b[it, s] = (behind + rs_b[it, s].astype(F32)).astype(BF16)
            rs_send_b(it, s).start()
            return carry

        if it == 0:
            lax.fori_loop(1, 7, rs_step, 0)
        else:
            lax.fori_loop(1, 4, rs_step, 0)
            norm_start(0, 3, norm_finish(0, 2))
            lax.fori_loop(4, 7, rs_step, 0)
        ahead = product(it, z + sg)
        own = product(it, z)
        rs_send_f(it, 6).wait_recv()
        rs_f[it, 7] = (ahead + rs_f[it, 7].astype(F32)).astype(BF16)
        rs_send_f(it, 7).start()
        rs_send_b(it, 6).wait_recv()
        own = own + rs_b[it, 7].astype(F32)
        if it == 1:
            scale = scale_of(norm_finish(0, 3))
        rs_send_f(it, 7).wait_recv()
        own = own + rs_f[it, 8].astype(F32)
        if it == 1:
            own = own * scale
        own = own.astype(BF16)

        yt[it, z] = own.astype(F32).T.astype(BF16)
        ag_send_f(it, 0).start()
        ag_send_b(it, 0).start()
        if it == 1:
            ex_i[0] = own[:64]
            ex_i[1] = own[64:]
            swap_i = remote(ex_i.at[1 - c], ex_i.at[2], es.at[0], er.at[0], partner)
            swap_i.start()
        add_products(it, [z], True)

        def ag_step(s, carry):
            ag_recv_f(it, s).wait_recv()
            ag_send_f(it, s + 1).start()
            ag_recv_b(it, s).wait_recv()

            @pl.when(s < 6)
            def _():
                ag_send_b(it, s + 1).start()

            add_products(it, [(z - sg * (s + 1) + 32) % 16, (z + sg * (s + 1) + 32) % 16], False)
            return carry

        lax.fori_loop(0, 7, ag_step, 0)
        if it == 1:
            swap_i.wait()
            image_ref[:, mine] = ex_i[c]
            image_ref[:, theirs] = ex_i[2]
        ag_recv_f(it, 7).wait_recv()
        add_products(it, [(z + 8) % 16], False)

        for j in range(BCD):
            blk = slice(j * BLOCK, (j + 1) * BLOCK)
            zero_half = acc[0, :, blk]
            one_half = acc[1, :, blk]
            pair = (
                jnp.where(lane, zero_half, pltpu.roll(one_half, 64, 1)).astype(BF16),
                jnp.where(lane, pltpu.roll(zero_half, 64, 1), one_half).astype(BF16),
            )
            for odd in (0, 1):
                xx, yy = divmod(2 * j + odd, 4)
                zc[it, 0, xx, yy // 2, yy % 2] = pair[odd][:64]
                zc[it, 1, yy, xx // 2, xx % 2] = pair[odd][64:]
        first, copies_a = rs4(it, 0, (0, 1))
        for h in (0, 1):
            for pos in range(4):
                value = first[h][pos // 2][pos % 2].astype(BF16)
                s2[it, h, pos, 0] = value[:32]
                s2[it, h, pos, 1] = value[32:]
        second, copies_b = rs4(it, 1, (1, 0))
        ranks = jnp.concatenate([second[0][0], second[0][1], second[1][0], second[1][1]], axis=0)
        rows = ranks.T
        squares = jnp.sum(rows * rows, axis=0, keepdims=True)
        if it == 0:
            low = rows.astype(BF16)
            bas[1, 0, x, y] = low[:64]
            bas[1, 1, x, y] = low[64:]
            copies_c = ag4_start(1, 0, (1, 0))
            norm_start(0, 0, squares)
            ag4_finish(1, 0, (1, 0), copies_c)
            copies_d = ag4_start(1, 1, (0, 1))
            norm_start(0, 1, norm_finish(0, 0))
            ag4_finish(1, 1, (0, 1), copies_d)
            for copies in copies_c + copies_d:
                for copy in copies.values():
                    copy.wait_send()
        else:
            norm_start(1, 0, squares)
            zfin[...] = rows
            norm_start(1, 1, norm_finish(1, 0))
            norm_start(1, 2, norm_finish(1, 1))
            norm_start(1, 3, norm_finish(1, 2))
            scale = scale_of(norm_finish(1, 3))
            low = (zfin[...] * scale).astype(BF16)
            ex_b[0] = low[:64]
            ex_b[1] = low[64:]
            swap_b = remote(ex_b.at[1 - c], ex_b.at[2], es.at[1], er.at[1], partner)
            swap_b.start()
            basis_ref[:, mine] = ex_b[c]
            swap_b.wait()
            basis_ref[:, theirs] = ex_b[2]
        for copies in copies_a + copies_b:
            for copy in copies.values():
                copy.wait_send()

    for it in (0, 1):

        def drain(s, carry):
            rs_send_f(it, s).wait_send()
            rs_send_b(it, s).wait_send()
            ag_send_f(it, s).wait_send()
            ag_send_b(it, s).wait_send()
            return carry

        lax.fori_loop(0, 7, drain, 0)
        rs_send_f(it, 7).wait_send()
        ag_send_f(it, 7).wait_send()
        for stage in range(4):
            for k in (1, 2, 3):
                norm_copy(it, stage, k).wait_send()


def shards(block_tiles, block_rows, block_cols, counts, start_basis):
    slots = jnp.arange(NB, dtype=jnp.int32)
    place = jnp.where(slots < counts[0, 0], block_rows[0] * BCD + block_cols[0], -1)
    hit = place[None, :] == jnp.arange(BRD * BCD, dtype=jnp.int32)[:, None]
    table = NB + jnp.sum(jnp.where(hit, slots[None, :] - NB, 0), axis=1, dtype=jnp.int32)
    table = table[None, :]
    start = start_basis.reshape(4, 4, 64, 2 * HALF)
    dma = pltpu.SemaphoreType.DMA
    vmem = pltpu.VMEM
    scratch = [
        pltpu.SMEM((1, 128), jnp.int32),
        vmem((1, 128), jnp.int32),
        vmem((NB + 1, BLOCK, BLOCK), BF16),
        vmem((NB + 1, BLOCK, BLOCK), BF16),
        vmem((2, BRD, BLOCK, 1024), BF16),
        vmem((2, 2, 4, 4, 64, HALF), BF16),
        vmem((2, 9, BLOCK, HALF), BF16),
        vmem((2, 8, BLOCK, HALF), BF16),
        vmem((2, 16, HALF, BLOCK), BF16),
        vmem((2, HALF, 1024), F32),
        vmem((2, 2, 4, 2, 2, 64, BLOCK), BF16),
        vmem((2, 2, 6, 2, 64, BLOCK), BF16),
        vmem((2, 2, 4, 2, 32, BLOCK), BF16),
        vmem((2, 2, 6, 32, BLOCK), BF16),
        vmem((BLOCK, HALF), F32),
        vmem((2, 4, 4, 8, HALF), F32),
        vmem((3, 64, HALF), BF16),
        vmem((3, 64, HALF), BF16),
        dma((3,)), dma((3,)), dma((3,)),
        dma((2, 2, 2, 8)), dma((2, 2, 2, 8)),
        dma((2, 2, 2, 2, 6)), dma((2, 2, 2, 2, 6)),
        dma((2, 4, 4)), dma((2, 4, 4)),
        dma((2,)), dma((2,)),
    ]
    anywhere = pl.BlockSpec(memory_space=pl.ANY)
    in_vmem = pl.BlockSpec(memory_space=pltpu.VMEM)
    return pl.pallas_call(
        kernel,
        out_shape=(
            jax.ShapeDtypeStruct((64, 2 * HALF), BF16),
            jax.ShapeDtypeStruct((64, 2 * HALF), BF16),
        ),
        in_specs=[pl.BlockSpec(memory_space=pltpu.SMEM), in_vmem, anywhere, anywhere],
        out_specs=(in_vmem, in_vmem),
        scratch_shapes=scratch,
        compiler_params=pltpu.CompilerParams(
            collective_id=0, has_side_effects=True, vmem_limit_bytes=48 * 1024 * 1024
        ),
    )(table, table, block_tiles, start)


def solution(mesh):
    in_specs = (
        P("row", "col", None, None), P("row", "col"), P("row", "col"), P("row", "col"), P("col", None),
    )
    out_specs = (P(("row", "col"), None), P(("col", "row"), None))
    return jax.shard_map(shards, mesh=mesh, in_specs=in_specs, out_specs=out_specs, check_vma=False)
```

time: 413 us -> 189 us (0.46)
  blocking collectives: 393 us -> 0 us
  Pallas kernels: 0 us -> 183 us
  matrix products: 13 us -> 0 us
    all_to_all x7 -> x0, blocking collectives: 293 us -> none  [the longest x4 162 us: summed_on_arrival(): lax.all_to_all(blocks, axis, split_axis=0, concat_axis=0, tiled=True)]
    pallas_call x0 -> x1, Pallas kernels: none -> 183 us  [shards(): pl.pallas_call(kernel, out_shape=(jax.ShapeDtypeStruct((64, 2 * HALF), BF...]
    psum x8 -> x0, blocking collectives: 99.5 us -> none  [one_axis_at_a_time(): value = lax.psum(value, axis)]
    dot_general x5 -> x0, matrix products: 13 us -> none  [the longest x2 7.11 us: shards(): lax.dot_general(dense_slab, image_slab, (((0,), (0,)), ((), ())), preferr...]
where the time goes in v1:
time: 189 us
  Pallas kernels  183 us (97%)
  local copies, waits for them, and re-layouts  4.01 us (2%)
    pallas_call x1, Pallas kernels, shards(): pl.pallas_call(kernel, out_shape=(jax.ShapeDtypeStruct((64, 2 * HALF), BF...  183 us
    unnamed x10, local copies, waits for them, and re-layouts  4.01 us

profile of v1, /device:TPU:1, one launch (start us, length us, event | category | flops | bytes accessed | tf_op | source)
XLA Modules:
  0.0 188.7 jit_solution(468438061014378312)
XLA Ops:
  1.3 0.0 copy-start.2
  1.3 0.0 copy-start.3
  1.3 0.6 copy-done.2
  1.9 0.0 copy-done.3
  2.0 0.1 select_reduce_fusion
  2.1 0.0 copy-start
  2.1 1.1 copy-done
  3.1 0.0 copy-start.1
  3.1 1.0 copy-done.1
  4.2 183.2 %shard_map.68 = (bf16[64,256]{1,0:T(8,128)(2,1)S(1)}, bf16[64,256]{1,0:T(8,128)(2,1)S(1)}) custom-call(s32[1,128]{1,0:T(1,128)S(1)} %add_bitcast_fusion.tab_ref.tabv_ref, s32[1,128]{1,0:T(1,128)S(1)} %add_bitcast_fusion.tab_ref.tabv_ref, bf16[1,20,128,128]{3,2,1,0:T(8,128)(2,1)S(1)} %copy-done, bf16[4,4,64,256]{3,2,1,0:T(8,128)(2,1)S(1)} %bitcast.7), custom_call_target="tpu_custom_call" | custom-call | tf_op jit(solution)/shard_map/pallas_call | solution.py:451
  187.4 0.6 copy.10
  188.1 0.6 copy.11
  (3 shorter events, 0.0 us)
Async XLA Ops:
  1.3 0.7 copy-start.2
  1.3 0.7 copy-start.3
  2.1 1.1 copy-start
  3.1 1.0 copy-start.1

commit v2 on v0

v2 whole, which is shorter than its diff:
```python
import functools

import jax
import jax.numpy as jnp
from jax import lax
from jax.experimental import pallas as pl
from jax.experimental.pallas import tpu as pltpu
from jax.sharding import PartitionSpec as P

BLOCK = 128
BRD = 16
BCD = 8
NB = 20
HALF = 128
TOTAL = 32768.0
F32 = jnp.float32
BF16 = jnp.bfloat16


TO_AGGREGATOR = ((8, 3), (7, 2), (-7, -2), (3, -2), (-3, 2), (6, 1), (-6, -1), (4, -1), (-4, 1))
TO_OWNER = ((5, 5), (-5, -5), (2, 2), (-2, -2), (1, 1), (-1, -1))
RELAYED = ((3, 3), (2, 2), (-2, -2), (1, 1), (-1, -1))


def kernel(
    rows_ref, cols_ref, counts_ref, tiles_ref, start_ref, image_ref, basis_ref,
    srows, scols, scount, tab, ptab, tabv, ptabv, tl_own, tl_in, dense, bas, zsnd, zrcv, yt, acc,
    zc, r1, s2, r2, zfin, nbuf, ex_i, ex_b,
    pre_send, pre_recv, loc_sem, zs, zr, xs, xr, ns, nr, es, er,
):
    row = lax.axis_index("row")
    col = lax.axis_index("col")
    x, y = row // 4, row % 4
    z, c = col // 2, col % 2
    sg = 1 - 2 * c

    def at(xx, yy, zz, cc):
        return (((xx + 4) % 4) * 4 + (yy + 4) % 4, ((zz + 16) % 16) * 2 + cc)

    def zpos(e):
        return (z + sg * e + 16) % 16

    def zdev(e):
        return (row, zpos(e) * 2 + c)

    def remote(src, dst, ssem, rsem, dev):
        return pltpu.make_async_remote_copy(
            src_ref=src, dst_ref=dst, send_sem=ssem, recv_sem=rsem,
            device_id=dev, device_id_type=pl.DeviceIdType.MESH,
        )

    partner = (row, z * 2 + 1 - c)
    pending = []

    def norm_dev(stage, k):
        if stage == 0:
            return ((row + k) % 16, col)
        return (row, ((z + k) % 16) * 2 + c)

    barrier = pltpu.get_barrier_semaphore()

    def greet(dev):
        pl.semaphore_signal(barrier, inc=1, device_id=dev, device_id_type=pl.DeviceIdType.MESH)

    greet(partner)

    def greet_line(k, carry):
        greet(norm_dev(1, k))
        greet(norm_dev(0, k))
        return carry

    lax.fori_loop(1, 16, greet_line, 0)

    local = [
        pltpu.make_async_copy(rows_ref, srows, loc_sem.at[0]),
        pltpu.make_async_copy(cols_ref, scols, loc_sem.at[1]),
        pltpu.make_async_copy(counts_ref, scount, loc_sem.at[2]),
        pltpu.make_async_copy(tiles_ref.at[0], tl_own.at[pl.ds(0, NB)], loc_sem.at[3]),
    ]
    for copy in local:
        copy.start()
    mine = pl.ds(pl.multiple_of(c * HALF, HALF), HALF)
    theirs = pl.ds(pl.multiple_of((1 - c) * HALF, HALF), HALF)
    own_start = pltpu.make_async_copy(start_ref.at[:, :, :, mine], bas.at[0, c], loc_sem.at[4])
    own_start.start()
    zero_tile = jnp.zeros((BLOCK, BLOCK), BF16)
    tl_own[NB] = zero_tile
    tl_in[NB] = zero_tile

    for copy in local[:3]:
        copy.wait()
    places = lax.broadcasted_iota(jnp.int32, (1, BRD * BCD), 1)
    slot_of = jnp.full((1, BRD * BCD), NB, jnp.int32)
    for slot in range(NB):
        place = jnp.where(slot < scount[0, 0], srows[0, slot] * BCD + scols[0, slot], -1)
        slot_of = jnp.where(places == place, slot, slot_of)
    tabv[...] = slot_of
    table_own = pltpu.make_async_copy(tabv, tab, loc_sem.at[5])
    table_own.start()

    pl.semaphore_wait(barrier, 31)
    pre = [
        remote(tabv, ptabv, pre_send.at[0], pre_recv.at[0], partner),
        remote(tiles_ref.at[0], tl_in.at[pl.ds(0, NB)], pre_send.at[1], pre_recv.at[1], partner),
        remote(start_ref.at[:, :, :, theirs], bas.at[0, c], pre_send.at[2], pre_recv.at[2], partner),
    ]
    for copy in pre:
        copy.start()

    def build(which, tl, table):
        def one_row(i, carry):
            for j in range(BCD):
                dense[which, i, :, j * BLOCK : (j + 1) * BLOCK] = tl[table[0, i * BCD + j]]
            return carry

        lax.fori_loop(0, BRD, one_row, 0)

    table_own.wait()
    local[3].wait()
    build(c, tl_own, tab)
    pre[0].wait_recv()
    table_in = pltpu.make_async_copy(ptabv, ptab, loc_sem.at[6])
    table_in.start()
    table_in.wait()
    pre[1].wait_recv()
    build(1 - c, tl_in, ptab)
    remote(start_ref.at[:, :, :, theirs], bas.at[0, 1 - c], pre_send.at[2], pre_recv.at[2], partner).wait_recv()
    own_start.wait()
    for copy in pre:
        copy.wait_send()

    def product(it, d):
        left = bas[it, 0].reshape(1024, HALF)
        right = bas[it, 1].reshape(1024, HALF)
        return jnp.dot(dense[0, d], left, preferred_element_type=F32) + jnp.dot(
            dense[1, d], right, preferred_element_type=F32
        )

    def rs_copy(it, m, e):
        return remote(zsnd.at[it, m], zrcv.at[it, m], zs.at[it, 0, m], zr.at[it, 0, m], zdev(e))

    def rs_launch(it, m, owner, e):
        zsnd[it, m] = product(it, zpos(owner)).astype(BF16)
        rs_copy(it, m, e).start()

    def rs_arrived(it, m):
        rs_copy(it, m, 1).wait_recv()
        return zrcv[it, m].astype(F32)

    def z_reduce(it, late):
        rs_launch(it, 0, 8, 3)

        def outer(k, carry):
            m = 1 + 4 * k
            rs_launch(it, m, 7 - k, 2 - k)
            rs_launch(it, m + 1, k - 7, k - 2)
            rs_launch(it, m + 2, 3 + k, k - 2)
            rs_launch(it, m + 3, -3 - k, 2 - k)
            return carry

        lax.fori_loop(0, 2, outer, 0)
        ahead = product(it, zpos(5))
        behind = product(it, zpos(-5))
        late()
        for m in (0, 1, 3, 5, 7):
            ahead = ahead + rs_arrived(it, m)
        zsnd[it, 9] = ahead.astype(BF16)
        rs_copy(it, 9, 5).start()
        for m in (2, 4, 6, 8):
            behind = behind + rs_arrived(it, m)
        zsnd[it, 10] = behind.astype(BF16)
        rs_copy(it, 10, -5).start()

        def near(k, carry):
            m = 11 + 2 * k
            rs_launch(it, m, 2 - k, 2 - k)
            rs_launch(it, m + 1, k - 2, k - 2)
            return carry

        lax.fori_loop(0, 2, near, 0)
        own = product(it, z)
        for m in (11, 12, 13, 14, 9, 10):
            own = own + rs_arrived(it, m)
        return own

    def z_drain(it, phase):
        def drain(m, carry):
            piece = zsnd.at[it, 0] if phase == 0 else yt.at[it, 0]
            remote(piece, piece, zs.at[it, phase, m], zr.at[it, phase, m], zdev(1)).wait_send()
            return carry

        lax.fori_loop(0, 15, drain, 0)

    def ag_copy(it, m, owner, e):
        piece = yt.at[it, zpos(owner)]
        return remote(piece, piece, zs.at[it, 1, m], zr.at[it, 1, m], zdev(e))

    def add_products(it, pieces, first):
        for which in (0, 1):
            for part in range(2):
                cols = pl.ds(part * 512, 512)
                total = None if first else acc[which, :, cols]
                for e in pieces:
                    p = zpos(e)
                    term = jnp.dot(yt[it, p], dense[which, p, :, cols], preferred_element_type=F32)
                    total = term if total is None else total + term
                acc[which, :, cols] = total

    def z_gather(it, late):
        for m, (_, e) in enumerate(TO_OWNER):
            ag_copy(it, m, 0, e).start()
        late()
        add_products(it, [0], True)
        ag_copy(it, 0, -5, 1).wait_recv()
        for i, (_, e) in enumerate(RELAYED):
            ag_copy(it, 6 + i, -5, e).start()
        ag_copy(it, 1, 5, 1).wait_recv()
        for i, (_, e) in enumerate(RELAYED[1:]):
            ag_copy(it, 11 + i, 5, e).start()
        for m, e in ((2, -2), (3, 2), (4, -1), (5, 1)):
            ag_copy(it, m, e, 1).wait_recv()
        add_products(it, [-5, 5, -2, 2, -1, 1], False)
        for m, e in ((9, -6), (10, -4), (13, 4), (14, 6)):
            ag_copy(it, m, e, 1).wait_recv()
        add_products(it, [-6, -4, 4, 6], False)
        for m, e in ((7, -7), (8, -3), (11, 3), (12, 7), (6, -8)):
            ag_copy(it, m, e, 1).wait_recv()
        add_products(it, [-7, -3, 3, 7, -8], False)

    def coord(axis):
        return x if axis == 0 else y

    def axis_dev(axis, k):
        if axis == 0:
            return at(x + k, y, z, c)
        return at(x, y + k, z, c)

    def xy_copy(it, phase, stage, h, k, axis, src, dst):
        i = (it, phase, stage, h, k - 1)
        return remote(src, dst, xs.at[i], xr.at[i], axis_dev(axis, k))

    def xy_reduce(it, stage, axes, buf, landing):
        copies = []
        for k in (2, 1, 3):
            for h in (0, 1):
                group = (coord(axes[h]) + k) % 4
                copy = xy_copy(it, 0, stage, h, k, axes[h], buf.at[it, h, group], landing.at[it, h, k - 1])
                copy.start()
                copies.append(copy)
        totals = [buf[it, h, coord(axes[h])].astype(F32) for h in (0, 1)]
        for i, copy in enumerate(copies):
            h, k = i % 2, (2, 1, 3)[i // 2]
            copy.wait_recv()
            totals[h] = totals[h] + landing[it, h, k - 1].astype(F32)
        pending.extend(copy.wait_send for copy in copies)
        return totals

    def piece_ref(it, h, stage, axis, g):
        if stage == 0:
            return bas.at[it, h, g, y] if axis == 0 else bas.at[it, h, x, g]
        return bas.at[it, h, g] if axis == 0 else bas.at[it, h, :, g]

    def xy_gather_start(it, stage, axes):
        copies = []
        for k in (2, 1, 3):
            for h in (0, 1):
                ref = piece_ref(it, h, stage, axes[h], coord(axes[h]))
                copy = xy_copy(it, 1, stage, h, k, axes[h], ref, ref)
                copy.start()
                copies.append(copy)
        pending.extend(copy.wait_send for copy in copies)

    def xy_gather_finish(it, stage, axes):
        for k in (1, 3, 2):
            for h in (0, 1):
                ref = piece_ref(it, h, stage, axes[h], (coord(axes[h]) + 4 - k) % 4)
                xy_copy(it, 1, stage, h, k, axes[h], ref, ref).wait_recv()

    def norm_copy(it, stage, k):
        return remote(
            nbuf.at[it, stage, 0], nbuf.at[it, stage, k], ns.at[it, stage, k], nr.at[it, stage, k],
            norm_dev(stage, k),
        )

    def norm_start(it, stage, value):
        nbuf[it, stage, 0] = jnp.broadcast_to(value, (8, HALF))

        def one(k, carry):
            norm_copy(it, stage, k).start()
            return carry

        lax.fori_loop(1, 16, one, 0)

        def drain_all():
            def drain(k, carry):
                norm_copy(it, stage, k).wait_send()
                return carry

            lax.fori_loop(1, 16, drain, 0)

        pending.append(drain_all)

    def norm_finish(it, stage):
        def one(k, carry):
            norm_copy(it, stage, k).wait_recv()
            return carry

        lax.fori_loop(1, 16, one, 0)
        return jnp.sum(nbuf[it, stage], axis=0)[0:1]

    def scale_of(total):
        return lax.rsqrt(total / TOTAL + 1e-06)

    lane = lax.broadcasted_iota(jnp.int32, (HALF, BLOCK), 1) < 64

    for it in (0, 1):
        def share_norm():
            if it == 1:
                norm_start(0, 1, norm_finish(0, 0))

        own = z_reduce(it, share_norm)
        pending.append(functools.partial(z_drain, it, 0))
        if it == 1:
            own = own * scale_of(norm_finish(0, 1))
        own = own.astype(BF16)

        yt[it, z] = own.astype(F32).T.astype(BF16)

        def share_image():
            if it == 1:
                ex_i[0] = own[:64]
                ex_i[1] = own[64:]
                remote(ex_i.at[1 - c], ex_i.at[2], es.at[0], er.at[0], partner).start()

        z_gather(it, share_image)
        pending.append(functools.partial(z_drain, it, 1))
        for j in range(BCD):
            blk = slice(j * BLOCK, (j + 1) * BLOCK)
            zero_half = acc[0, :, blk]
            one_half = acc[1, :, blk]
            pair = (
                jnp.where(lane, zero_half, pltpu.roll(one_half, 64, 1)).astype(BF16),
                jnp.where(lane, pltpu.roll(zero_half, 64, 1), one_half).astype(BF16),
            )
            for odd in (0, 1):
                xx, yy = divmod(2 * j + odd, 4)
                zc[it, 0, xx, yy] = pair[odd][:64]
                zc[it, 1, yy, xx] = pair[odd][64:]
        first = xy_reduce(it, 0, (0, 1), zc, r1)
        for h in (0, 1):
            s2[it, h] = first[h].astype(BF16)
        second = xy_reduce(it, 1, (1, 0), s2, r2)
        rows = jnp.concatenate(second, axis=0).T
        squares = jnp.sum(rows * rows, axis=0, keepdims=True)
        if it == 0:
            low = rows.astype(BF16)
            bas[1, 0, x, y] = low[:64]
            bas[1, 1, x, y] = low[64:]
            xy_gather_start(1, 0, (1, 0))
            norm_start(0, 0, squares)
            xy_gather_finish(1, 0, (1, 0))
            xy_gather_start(1, 1, (0, 1))
            xy_gather_finish(1, 1, (0, 1))
        else:
            norm_start(1, 0, squares)
            zfin[...] = rows
            remote(ex_i.at[1 - c], ex_i.at[2], es.at[0], er.at[0], partner).wait()
            image_ref[:, mine] = ex_i[c]
            image_ref[:, theirs] = ex_i[2]
            norm_start(1, 1, norm_finish(1, 0))
            low = (zfin[...] * scale_of(norm_finish(1, 1))).astype(BF16)
            ex_b[0] = low[:64]
            ex_b[1] = low[64:]
            swap = remote(ex_b.at[1 - c], ex_b.at[2], es.at[1], er.at[1], partner)
            swap.start()
            basis_ref[:, mine] = ex_b[c]
            swap.wait()
            basis_ref[:, theirs] = ex_b[2]

    for drain in pending:
        drain()


def shards(block_tiles, block_rows, block_cols, counts, start_basis):
    start = start_basis.reshape(4, 4, 64, 2 * HALF)
    dma = pltpu.SemaphoreType.DMA
    vmem = pltpu.VMEM
    smem = pltpu.SMEM
    scratch = [
        smem((1, NB), jnp.int32), smem((1, NB), jnp.int32), smem((1, 1), jnp.int32),
        smem((1, 128), jnp.int32), smem((1, 128), jnp.int32),
        vmem((1, 128), jnp.int32), vmem((1, 128), jnp.int32),
        vmem((NB + 1, BLOCK, BLOCK), BF16),
        vmem((NB + 1, BLOCK, BLOCK), BF16),
        vmem((2, BRD, BLOCK, 1024), BF16),
        vmem((2, 2, 4, 4, 64, HALF), BF16),
        vmem((2, 15, BLOCK, HALF), BF16),
        vmem((2, 15, BLOCK, HALF), BF16),
        vmem((2, 16, HALF, BLOCK), BF16),
        vmem((2, HALF, 1024), F32),
        vmem((2, 2, 4, 4, 64, BLOCK), BF16),
        vmem((2, 2, 3, 4, 64, BLOCK), BF16),
        vmem((2, 2, 4, 64, BLOCK), BF16),
        vmem((2, 2, 3, 64, BLOCK), BF16),
        vmem((BLOCK, HALF), F32),
        vmem((2, 2, 16, 8, HALF), F32),
        vmem((3, 64, HALF), BF16),
        vmem((3, 64, HALF), BF16),
        dma((3,)), dma((3,)), dma((7,)),
        dma((2, 2, 15)), dma((2, 2, 15)),
        dma((2, 2, 2, 2, 3)), dma((2, 2, 2, 2, 3)),
        dma((2, 2, 16)), dma((2, 2, 16)),
        dma((2,)), dma((2,)),
    ]
    anywhere = pl.BlockSpec(memory_space=pl.ANY)
    in_vmem = pl.BlockSpec(memory_space=pltpu.VMEM)
    return pl.pallas_call(
        kernel,
        out_shape=(
            jax.ShapeDtypeStruct((64, 2 * HALF), BF16),
            jax.ShapeDtypeStruct((64, 2 * HALF), BF16),
        ),
        in_specs=[anywhere] * 5,
        out_specs=(in_vmem, in_vmem),
        scratch_shapes=scratch,
        compiler_params=pltpu.CompilerParams(
            collective_id=0, has_side_effects=True, vmem_limit_bytes=48 * 1024 * 1024
        ),
    )(block_rows, block_cols, counts, block_tiles, start)


def solution(mesh):
    in_specs = (
        P("row", "col", None, None), P("row", "col"), P("row", "col"), P("row", "col"), P("col", None),
    )
    out_specs = (P(("row", "col"), None), P(("col", "row"), None))
    return jax.shard_map(shards, mesh=mesh, in_specs=in_specs, out_specs=out_specs, check_vma=False)
```

time: 413 us -> 133 us (0.32)
  blocking collectives: 393 us -> 0 us
  Pallas kernels: 0 us -> 127 us
  matrix products: 13 us -> 0 us
    all_to_all x7 -> x0, blocking collectives: 293 us -> none  [the longest x4 162 us: summed_on_arrival(): lax.all_to_all(blocks, axis, split_axis=0, concat_axis=0, tiled=True)]
    pallas_call x0 -> x1, Pallas kernels: none -> 127 us  [shards(): pl.pallas_call(kernel, out_shape=(jax.ShapeDtypeStruct((64, 2 * HALF), BF...]
    psum x8 -> x0, blocking collectives: 99.5 us -> none  [one_axis_at_a_time(): value = lax.psum(value, axis)]
    dot_general x5 -> x0, matrix products: 13 us -> none  [the longest x2 7.11 us: shards(): lax.dot_general(dense_slab, image_slab, (((0,), (0,)), ((), ())), preferr...]
where the time goes in v2:
time: 133 us; the launch traced here: 132 us
  Pallas kernels  127 us (95%)
  local copies, waits for them, and re-layouts  4.02 us (3%)
    pallas_call x1, Pallas kernels, shards(): pl.pallas_call(kernel, out_shape=(jax.ShapeDtypeStruct((64, 2 * HALF), BF...  127 us
    unnamed x10, local copies, waits for them, and re-layouts  4.02 us

profile of v2, /device:TPU:1, one launch (start us, length us, event | category | flops | bytes accessed | tf_op | source)
XLA Modules:
  0.0 132.3 jit_solution(2541680044580480724)
XLA Ops:
  1.3 0.0 copy-start.2
  1.3 0.0 copy-start.3
  1.3 0.6 copy-done.2
  1.9 0.0 copy-done.3
  1.9 0.0 copy-start
  2.0 1.1 copy-done
  3.0 0.0 copy-start.1
  3.0 1.0 copy-done.1
  4.1 127.0 %shard_map.68 = (bf16[64,256]{1,0:T(8,128)(2,1)S(1)}, bf16[64,256]{1,0:T(8,128)(2,1)S(1)}) custom-call(s32[1,20]{1,0:T(1,128)S(1)} %copy-done.2, s32[1,20]{1,0:T(1,128)S(1)} %copy-done.3, s32[1,1]{1,0:T(1,128)S(6)} %copy.9.counts_ref, bf16[1,20,128,128]{3,2,1,0:T(8,128)(2,1)S(1)} %copy-done, bf16[4,4,64,256]{3,2,1,0:T(8,128)(2,1)S(1)} %bitcast.1), custom_call_target="tpu_custom_call" | custom-call | tf_op jit(solution)/shard_map/pallas_call | solution.py:417
  131.0 0.6 copy.10
  131.7 0.6 copy.11
Async XLA Ops:
  1.3 0.7 copy-start.2
  1.3 0.7 copy-start.3
  1.9 1.1 copy-start
  3.0 1.0 copy-start.1

commit v3 on v2

--- a/solution.py
+++ b/solution.py
@@ -17,9 +17,8 @@
 BF16 = jnp.bfloat16
 
 
-TO_AGGREGATOR = ((8, 3), (7, 2), (-7, -2), (3, -2), (-3, 2), (6, 1), (-6, -1), (4, -1), (-4, 1))
-TO_OWNER = ((5, 5), (-5, -5), (2, 2), (-2, -2), (1, 1), (-1, -1))
-RELAYED = ((3, 3), (2, 2), (-2, -2), (1, 1), (-1, -1))
+TO_OWNER = (5, -5, 2, -2, 1, -1)
+RELAYED = (3, 2, -2, 1, -1)
 
 
 def kernel(
@@ -65,11 +64,13 @@
     greet(partner)
 
     def greet_line(k, carry):
-        greet(norm_dev(1, k))
-        greet(norm_dev(0, k))
+        greet(zdev(k))
+        greet(zdev(-k))
+        greet(at(x + k, y, z, c))
+        greet(at(x, y + k, z, c))
         return carry
 
-    lax.fori_loop(1, 16, greet_line, 0)
+    lax.fori_loop(1, 4, greet_line, 0)
 
     local = [
         pltpu.make_async_copy(rows_ref, srows, loc_sem.at[0]),
@@ -98,7 +99,7 @@
     table_own = pltpu.make_async_copy(tabv, tab, loc_sem.at[5])
     table_own.start()
 
-    pl.semaphore_wait(barrier, 31)
+    pl.semaphore_wait(barrier, 13)
     pre = [
         remote(tabv, ptabv, pre_send.at[0], pre_recv.at[0], partner),
         remote(tiles_ref.at[0], tl_in.at[pl.ds(0, NB)], pre_send.at[1], pre_recv.at[1], partner),
@@ -136,95 +137,84 @@
             dense[1, d], right, preferred_element_type=F32
         )
 
-    def rs_copy(it, m, e):
-        return remote(zsnd.at[it, m], zrcv.at[it, m], zs.at[it, 0, m], zr.at[it, 0, m], zdev(e))
-
-    def rs_launch(it, m, owner, e):
+    def rs_launch(it, m, group, owner, e):
         zsnd[it, m] = product(it, zpos(owner)).astype(BF16)
-        rs_copy(it, m, e).start()
-
-    def rs_arrived(it, m):
-        rs_copy(it, m, 1).wait_recv()
-        return zrcv[it, m].astype(F32)
+        rs_send(it, m, group, e)
+
+    def rs_send(it, m, group, e):
+        remote(zsnd.at[it, m], zrcv.at[it, m], zs.at[it, 0], zr.at[it, group], zdev(e)).start()
+
+    def rs_arrived(it, group, begin, count):
+        part = zrcv.at[it, pl.ds(begin, count)]
+        remote(part, part, zs.at[it, 0], zr.at[it, group], zdev(1)).wait_recv()
+        return jnp.sum(zrcv[it, begin : begin + count].astype(F32), axis=0)
 
     def z_reduce(it, late):
-        rs_launch(it, 0, 8, 3)
+        rs_launch(it, 0, 0, 8, 3)
 
         def outer(k, carry):
-            m = 1 + 4 * k
-            rs_launch(it, m, 7 - k, 2 - k)
-            rs_launch(it, m + 1, k - 7, k - 2)
-            rs_launch(it, m + 2, 3 + k, k - 2)
-            rs_launch(it, m + 3, -3 - k, 2 - k)
+            m = 2 * k
+            rs_launch(it, m + 1, 0, 7 - k, 2 - k)
+            rs_launch(it, m + 5, 1, k - 7, k - 2)
+            rs_launch(it, m + 2, 0, 3 + k, k - 2)
+            rs_launch(it, m + 6, 1, -3 - k, 2 - k)
             return carry
 
         lax.fori_loop(0, 2, outer, 0)
+
+        def near(k, carry):
+            m = 11 + 2 * k
+            rs_launch(it, m, 2, 2 - k, 2 - k)
+            rs_launch(it, m + 1, 2, k - 2, k - 2)
+            return carry
+
+        lax.fori_loop(0, 2, near, 0)
         ahead = product(it, zpos(5))
         behind = product(it, zpos(-5))
+        own = product(it, z)
         late()
-        for m in (0, 1, 3, 5, 7):
-            ahead = ahead + rs_arrived(it, m)
-        zsnd[it, 9] = ahead.astype(BF16)
-        rs_copy(it, 9, 5).start()
-        for m in (2, 4, 6, 8):
-            behind = behind + rs_arrived(it, m)
-        zsnd[it, 10] = behind.astype(BF16)
-        rs_copy(it, 10, -5).start()
-
-        def near(k, carry):
-            m = 11 + 2 * k
-            rs_launch(it, m, 2 - k, 2 - k)
-            rs_launch(it, m + 1, k - 2, k - 2)
-            return carry
-
-        lax.fori_loop(0, 2, near, 0)
-        own = product(it, z)
-        for m in (11, 12, 13, 14, 9, 10):
-            own = own + rs_arrived(it, m)
-        return own
+        zsnd[it, 9] = (ahead + rs_arrived(it, 0, 0, 5)).astype(BF16)
+        rs_send(it, 9, 2, 5)
+        zsnd[it, 10] = (behind + rs_arrived(it, 1, 5, 4)).astype(BF16)
+        rs_send(it, 10, 2, -5)
+        return own + rs_arrived(it, 2, 9, 6)
 
     def z_drain(it, phase):
-        def drain(m, carry):
-            piece = zsnd.at[it, 0] if phase == 0 else yt.at[it, 0]
-            remote(piece, piece, zs.at[it, phase, m], zr.at[it, phase, m], zdev(1)).wait_send()
-            return carry
-
-        lax.fori_loop(0, 15, drain, 0)
-
-    def ag_copy(it, m, owner, e):
+        part = (zsnd if phase == 0 else yt).at[it, pl.ds(0, 15)]
+        remote(part, part, zs.at[it, phase], zr.at[it, 0], zdev(1)).wait_send()
+
+    def ag_send(it, group, owner, e):
         piece = yt.at[it, zpos(owner)]
-        return remote(piece, piece, zs.at[it, 1, m], zr.at[it, 1, m], zdev(e))
+        remote(piece, piece, zs.at[it, 1], zr.at[it, group], zdev(e)).start()
+
+    def ag_arrived(it, group, count):
+        part = yt.at[it, pl.ds(0, count)]
+        remote(part, part, zs.at[it, 1], zr.at[it, group], zdev(1)).wait_recv()
 
     def add_products(it, pieces, first):
         for which in (0, 1):
             for part in range(2):
                 cols = pl.ds(part * 512, 512)
-                total = None if first else acc[which, :, cols]
-                for e in pieces:
-                    p = zpos(e)
-                    term = jnp.dot(yt[it, p], dense[which, p, :, cols], preferred_element_type=F32)
-                    total = term if total is None else total + term
-                acc[which, :, cols] = total
+                left = jnp.concatenate([yt[it, zpos(e)] for e in pieces], axis=1)
+                right = jnp.concatenate([dense[which, zpos(e), :, cols] for e in pieces], axis=0)
+                term = jnp.dot(left, right, preferred_element_type=F32)
+                acc[which, :, cols] = term if first else acc[which, :, cols] + term
 
     def z_gather(it, late):
-        for m, (_, e) in enumerate(TO_OWNER):
-            ag_copy(it, m, 0, e).start()
+        for i, e in enumerate(TO_OWNER):
+            ag_send(it, 3 + min(i, 2), 0, e)
         late()
-        add_products(it, [0], True)
-        ag_copy(it, 0, -5, 1).wait_recv()
-        for i, (_, e) in enumerate(RELAYED):
-            ag_copy(it, 6 + i, -5, e).start()
-        ag_copy(it, 1, 5, 1).wait_recv()
-        for i, (_, e) in enumerate(RELAYED[1:]):
-            ag_copy(it, 11 + i, 5, e).start()
-        for m, e in ((2, -2), (3, 2), (4, -1), (5, 1)):
-            ag_copy(it, m, e, 1).wait_recv()
-        add_products(it, [-5, 5, -2, 2, -1, 1], False)
-        for m, e in ((9, -6), (10, -4), (13, 4), (14, 6)):
-            ag_copy(it, m, e, 1).wait_recv()
+        ag_arrived(it, 3, 1)
+        for e in RELAYED:
+            ag_send(it, 6 if abs(e) == 1 else 7, -5, e)
+        ag_arrived(it, 4, 1)
+        for e in RELAYED[1:]:
+            ag_send(it, 6 if abs(e) == 1 else 7, 5, e)
+        ag_arrived(it, 5, 4)
+        add_products(it, [-5, 5, -2, 2, -1, 1, 0], True)
+        ag_arrived(it, 6, 4)
         add_products(it, [-6, -4, 4, 6], False)
-        for m, e in ((7, -7), (8, -3), (11, 3), (12, 7), (6, -8)):
-            ag_copy(it, m, e, 1).wait_recv()
+        ag_arrived(it, 7, 5)
         add_products(it, [-7, -3, 3, 7, -8], False)
 
     def coord(axis):
@@ -236,23 +226,26 @@
         return at(x, y + k, z, c)
 
     def xy_copy(it, phase, stage, h, k, axis, src, dst):
-        i = (it, phase, stage, h, k - 1)
-        return remote(src, dst, xs.at[i], xr.at[i], axis_dev(axis, k))
+        p = it * (2 - phase)
+        return remote(src, dst, xs.at[p, stage], xr.at[p, stage, h], axis_dev(axis, k))
+
+    def xy_drain(it, phase, stage, part):
+        xy_copy(it, phase, stage, 0, 1, 0, part, part).wait_send()
 
     def xy_reduce(it, stage, axes, buf, landing):
-        copies = []
         for k in (2, 1, 3):
             for h in (0, 1):
                 group = (coord(axes[h]) + k) % 4
-                copy = xy_copy(it, 0, stage, h, k, axes[h], buf.at[it, h, group], landing.at[it, h, k - 1])
-                copy.start()
-                copies.append(copy)
-        totals = [buf[it, h, coord(axes[h])].astype(F32) for h in (0, 1)]
-        for i, copy in enumerate(copies):
-            h, k = i % 2, (2, 1, 3)[i // 2]
-            copy.wait_recv()
-            totals[h] = totals[h] + landing[it, h, k - 1].astype(F32)
-        pending.extend(copy.wait_send for copy in copies)
+                xy_copy(it, 0, stage, h, k, axes[h], buf.at[it, h, group], landing.at[it, h, k - 1]).start()
+        totals = []
+        for h in (0, 1):
+            part = landing.at[it, h]
+            xy_copy(it, 0, stage, h, 1, 0, part, part).wait_recv()
+            total = buf[it, h, coord(axes[h])].astype(F32)
+            for k in range(3):
+                total = total + landing[it, h, k].astype(F32)
+            totals.append(total)
+        pending.append(functools.partial(xy_drain, it, 0, stage, buf.at[it, :, pl.ds(0, 3)]))
         return totals
 
     def piece_ref(it, h, stage, axis, g):
@@ -260,52 +253,37 @@
             return bas.at[it, h, g, y] if axis == 0 else bas.at[it, h, x, g]
         return bas.at[it, h, g] if axis == 0 else bas.at[it, h, :, g]
 
-    def xy_gather_start(it, stage, axes):
-        copies = []
+    def three(it, stage, h):
+        return bas.at[it, h, 0, pl.ds(0, 3)] if stage == 0 else bas.at[it, h, pl.ds(0, 3)]
+
+    def xy_gather(it, stage, axes, late):
         for k in (2, 1, 3):
             for h in (0, 1):
                 ref = piece_ref(it, h, stage, axes[h], coord(axes[h]))
-                copy = xy_copy(it, 1, stage, h, k, axes[h], ref, ref)
-                copy.start()
-                copies.append(copy)
-        pending.extend(copy.wait_send for copy in copies)
-
-    def xy_gather_finish(it, stage, axes):
-        for k in (1, 3, 2):
-            for h in (0, 1):
-                ref = piece_ref(it, h, stage, axes[h], (coord(axes[h]) + 4 - k) % 4)
-                xy_copy(it, 1, stage, h, k, axes[h], ref, ref).wait_recv()
-
-    def norm_copy(it, stage, k):
-        return remote(
-            nbuf.at[it, stage, 0], nbuf.at[it, stage, k], ns.at[it, stage, k], nr.at[it, stage, k],
-            norm_dev(stage, k),
-        )
+                xy_copy(it, 1, stage, h, k, axes[h], ref, ref).start()
+        pending.append(functools.partial(xy_drain, it, 1, stage, three(it, stage, slice(None))))
+        late()
+        for h in (0, 1):
+            part = three(it, stage, h)
+            xy_copy(it, 1, stage, h, 1, 0, part, part).wait_recv()
+
+    def norm_copy(it, stage, src, dst, k):
+        return remote(src, dst, ns.at[it, stage], nr.at[it, stage], norm_dev(stage, k))
 
     def norm_start(it, stage, value):
         nbuf[it, stage, 0] = jnp.broadcast_to(value, (8, HALF))
 
         def one(k, carry):
-            norm_copy(it, stage, k).start()
+            norm_copy(it, stage, nbuf.at[it, stage, 0], nbuf.at[it, stage, k], k).start()
             return carry
 
         lax.fori_loop(1, 16, one, 0)
-
-        def drain_all():
-            def drain(k, carry):
-                norm_copy(it, stage, k).wait_send()
-                return carry
-
-            lax.fori_loop(1, 16, drain, 0)
-
-        pending.append(drain_all)
+        rest = nbuf.at[it, stage, pl.ds(1, 15)]
+        pending.append(norm_copy(it, stage, rest, rest, 1).wait_send)
 
     def norm_finish(it, stage):
-        def one(k, carry):
-            norm_copy(it, stage, k).wait_recv()
-            return carry
-
-        lax.fori_loop(1, 16, one, 0)
+        rest = nbuf.at[it, stage, pl.ds(1, 15)]
+        norm_copy(it, stage, rest, rest, 1).wait_recv()
         return jnp.sum(nbuf[it, stage], axis=0)[0:1]
 
     def scale_of(total):
@@ -356,11 +334,8 @@
             low = rows.astype(BF16)
             bas[1, 0, x, y] = low[:64]
             bas[1, 1, x, y] = low[64:]
-            xy_gather_start(1, 0, (1, 0))
-            norm_start(0, 0, squares)
-            xy_gather_finish(1, 0, (1, 0))
-            xy_gather_start(1, 1, (0, 1))
-            xy_gather_finish(1, 1, (0, 1))
+            xy_gather(1, 0, (1, 0), functools.partial(norm_start, 0, 0, squares))
+            xy_gather(1, 1, (0, 1), lambda: None)
         else:
             norm_start(1, 0, squares)
             zfin[...] = rows
@@ -407,9 +382,9 @@
         vmem((3, 64, HALF), BF16),
         vmem((3, 64, HALF), BF16),
         dma((3,)), dma((3,)), dma((7,)),
-        dma((2, 2, 15)), dma((2, 2, 15)),
-        dma((2, 2, 2, 2, 3)), dma((2, 2, 2, 2, 3)),
-        dma((2, 2, 16)), dma((2, 2, 16)),
+        dma((2, 2)), dma((2, 8)),
+        dma((3, 2)), dma((3, 2, 2)),
+        dma((2, 2)), dma((2, 2)),
         dma((2,)), dma((2,)),
     ]
     anywhere = pl.BlockSpec(memory_space=pl.ANY)
@@ -424,7 +399,7 @@
         out_specs=(in_vmem, in_vmem),
         scratch_shapes=scratch,
         compiler_params=pltpu.CompilerParams(
-            collective_id=0, has_side_effects=True, vmem_limit_bytes=48 * 1024 * 1024
+            collective_id=0, has_side_effects=True, vmem_limit_bytes=63 * 1024 * 1024
         ),
     )(block_rows, block_cols, counts, block_tiles, start)
 

time: 133 us -> 123 us (0.925)
  Pallas kernels: 127 us -> 120 us
  local copies, waits for them, and re-layouts: 4.02 us -> 2 us
    pallas_call x1, Pallas kernels: 127 us -> 120 us  [shards(): pl.pallas_call(kernel, out_shape=(jax.ShapeDtypeStruct((64, 2 * HALF), BF...]
    unnamed x10 -> x4, local copies, waits for them, and re-layouts: 4.02 us -> 2 us
where the time goes in v3:
time: 123 us
  Pallas kernels  120 us (98%)
  local copies, waits for them, and re-layouts  2 us (2%)
  between operations  1.29 us (1%)
    pallas_call x1, Pallas kernels, shards(): pl.pallas_call(kernel, out_shape=(jax.ShapeDtypeStruct((64, 2 * HALF), BF...  120 us

profile of v3, /device:TPU:1, one launch (start us, length us, event | category | flops | bytes accessed | tf_op | source)
XLA Modules:
  0.0 122.8 jit_solution(1536941210557002427)
XLA Ops:
  1.3 119.5 %shard_map.68 = (bf16[64,256]{1,0:T(8,128)(2,1)}, bf16[64,256]{1,0:T(8,128)(2,1)}) custom-call(s32[1,20]{1,0:T(1,128)} %rows_ref.1, s32[1,20]{1,0:T(1,128)} %cols_ref.1, s32[1,1]{1,0:T(1,128)S(6)} %copy.9.counts_ref, bf16[1,20,128,128]{3,2,1,0:T(8,128)(2,1)} %tiles_ref.1, bf16[4,4,64,256]{3,2,1,0:T(8,128)(2,1)} %bitcast.1), custom_call_target="tpu_custom_call" | custom-call | tf_op jit(solution)/shard_map/pallas_call | solution.py:392
  120.8 0.0 copy-start
  120.8 1.4 %copy.10 = bf16[64,256]{1,0:T(8,128)(2,1)} copy(bf16[64,256]{1,0:T(8,128)(2,1)} %get-tuple-element.4) | data formatting | bytes 65536
  122.2 0.0 copy-done
  122.2 0.6 copy.11
Async XLA Ops:
  120.8 1.4 %copy-start = (bf16[64,256]{1,0:T(8,128)(2,1)S(1)}, bf16[64,256]{1,0:T(8,128)(2,1)}, u32[]{:S(2)}) copy-start(bf16[64,256]{1,0:T(8,128)(2,1)} %get-tuple-element.5) | copy-start | bytes 98308

commit v4 on v3

--- a/solution.py
+++ b/solution.py
@@ -17,15 +17,15 @@
 BF16 = jnp.bfloat16
 
 
-TO_OWNER = (5, -5, 2, -2, 1, -1)
-RELAYED = (3, 2, -2, 1, -1)
+TO_OWNER = (5, -5, 3, -3, 2, -2, 1, -1)
+RELAYED = (3, 2, 1, -1)
 
 
 def kernel(
     rows_ref, cols_ref, counts_ref, tiles_ref, start_ref, image_ref, basis_ref,
     srows, scols, scount, tab, ptab, tabv, ptabv, tl_own, tl_in, dense, bas, zsnd, zrcv, yt, acc,
     zc, r1, s2, r2, zfin, nbuf, ex_i, ex_b,
-    pre_send, pre_recv, loc_sem, zs, zr, xs, xr, ns, nr, es, er,
+    pre_send, pre_recv, loc_sem, zs, zr, xs, xr, ns, nr, es, er, turn,
 ):
     row = lax.axis_index("row")
     col = lax.axis_index("col")
@@ -209,13 +209,13 @@
             ag_send(it, 6 if abs(e) == 1 else 7, -5, e)
         ag_arrived(it, 4, 1)
         for e in RELAYED[1:]:
-            ag_send(it, 6 if abs(e) == 1 else 7, 5, e)
-        ag_arrived(it, 5, 4)
-        add_products(it, [-5, 5, -2, 2, -1, 1, 0], True)
+            ag_send(it, 6 if abs(e) == 1 else 7, 5, -e)
+        ag_arrived(it, 5, 6)
+        add_products(it, [-5, 5, -3, 3, -2, 2, -1, 1, 0], True)
         ag_arrived(it, 6, 4)
         add_products(it, [-6, -4, 4, 6], False)
-        ag_arrived(it, 7, 5)
-        add_products(it, [-7, -3, 3, 7, -8], False)
+        ag_arrived(it, 7, 3)
+        add_products(it, [-7, 7, -8], False)
 
     def coord(axis):
         return x if axis == 0 else y
@@ -232,21 +232,29 @@
     def xy_drain(it, phase, stage, part):
         xy_copy(it, phase, stage, 0, 1, 0, part, part).wait_send()
 
-    def xy_reduce(it, stage, axes, buf, landing):
-        for k in (2, 1, 3):
-            for h in (0, 1):
-                group = (coord(axes[h]) + k) % 4
-                xy_copy(it, 0, stage, h, k, axes[h], buf.at[it, h, group], landing.at[it, h, k - 1]).start()
-        totals = []
-        for h in (0, 1):
+    def xy_reduce(it):
+        def send(stage, h, buf, landing):
+            axis = (h + stage) % 2
+            for k in (2, 1, 3):
+                group = (coord(axis) + k) % 4
+                xy_copy(it, 0, stage, h, k, axis, buf.at[it, h, group], landing.at[it, h, k - 1]).start()
+
+        def total(stage, h, buf, landing):
             part = landing.at[it, h]
             xy_copy(it, 0, stage, h, 1, 0, part, part).wait_recv()
-            total = buf[it, h, coord(axes[h])].astype(F32)
+            value = buf[it, h, coord((h + stage) % 2)].astype(F32)
             for k in range(3):
-                total = total + landing[it, h, k].astype(F32)
-            totals.append(total)
-        pending.append(functools.partial(xy_drain, it, 0, stage, buf.at[it, :, pl.ds(0, 3)]))
-        return totals
+                value = value + landing[it, h, k].astype(F32)
+            return value
+
+        for h in range(4):
+            send(0, h, zc, r1)
+        for h in range(4):
+            s2[it, h] = total(0, h, zc, r1).astype(BF16)
+            send(1, h, s2, r2)
+        pending.append(functools.partial(xy_drain, it, 0, 0, zc.at[it, :, pl.ds(0, 3)]))
+        pending.append(functools.partial(xy_drain, it, 0, 1, s2.at[it, :, pl.ds(0, 3)]))
+        return [total(1, h, s2, r2) for h in range(4)]
 
     def piece_ref(it, h, stage, axis, g):
         if stage == 0:
@@ -289,6 +297,15 @@
     def scale_of(total):
         return lax.rsqrt(total / TOTAL + 1e-06)
 
+    def give_turn():
+        @pl.when(c == 0)
+        def _():
+            pl.semaphore_signal(turn, inc=1, device_id=partner, device_id_type=pl.DeviceIdType.MESH)
+
+    @pl.when(c == 1)
+    def _():
+        pl.semaphore_wait(turn, 1)
+
     lane = lax.broadcasted_iota(jnp.int32, (HALF, BLOCK), 1) < 64
 
     for it in (0, 1):
@@ -297,6 +314,8 @@
                 norm_start(0, 1, norm_finish(0, 0))
 
         own = z_reduce(it, share_norm)
+        if it == 0:
+            give_turn()
         pending.append(functools.partial(z_drain, it, 0))
         if it == 1:
             own = own * scale_of(norm_finish(0, 1))
@@ -322,12 +341,10 @@
             )
             for odd in (0, 1):
                 xx, yy = divmod(2 * j + odd, 4)
-                zc[it, 0, xx, yy] = pair[odd][:64]
-                zc[it, 1, yy, xx] = pair[odd][64:]
-        first = xy_reduce(it, 0, (0, 1), zc, r1)
-        for h in (0, 1):
-            s2[it, h] = first[h].astype(BF16)
-        second = xy_reduce(it, 1, (1, 0), s2, r2)
+                for h in range(4):
+                    xy = (yy, xx) if h % 2 else (xx, yy)
+                    zc[it, h, xy[0], xy[1]] = pair[odd][32 * h : 32 * h + 32]
+        second = xy_reduce(it)
         rows = jnp.concatenate(second, axis=0).T
         squares = jnp.sum(rows * rows, axis=0, keepdims=True)
         if it == 0:
@@ -373,19 +390,20 @@
         vmem((2, 15, BLOCK, HALF), BF16),
         vmem((2, 16, HALF, BLOCK), BF16),
         vmem((2, HALF, 1024), F32),
-        vmem((2, 2, 4, 4, 64, BLOCK), BF16),
-        vmem((2, 2, 3, 4, 64, BLOCK), BF16),
-        vmem((2, 2, 4, 64, BLOCK), BF16),
-        vmem((2, 2, 3, 64, BLOCK), BF16),
+        vmem((2, 4, 4, 4, 32, BLOCK), BF16),
+        vmem((2, 4, 3, 4, 32, BLOCK), BF16),
+        vmem((2, 4, 4, 32, BLOCK), BF16),
+        vmem((2, 4, 3, 32, BLOCK), BF16),
         vmem((BLOCK, HALF), F32),
         vmem((2, 2, 16, 8, HALF), F32),
         vmem((3, 64, HALF), BF16),
         vmem((3, 64, HALF), BF16),
         dma((3,)), dma((3,)), dma((7,)),
         dma((2, 2)), dma((2, 8)),
-        dma((3, 2)), dma((3, 2, 2)),
+        dma((3, 2)), dma((3, 2, 4)),
         dma((2, 2)), dma((2, 2)),
         dma((2,)), dma((2,)),
+        pltpu.SemaphoreType.REGULAR,
     ]
     anywhere = pl.BlockSpec(memory_space=pl.ANY)
     in_vmem = pl.BlockSpec(memory_space=pltpu.VMEM)
@@ -399,7 +417,7 @@
         out_specs=(in_vmem, in_vmem),
         scratch_shapes=scratch,
         compiler_params=pltpu.CompilerParams(
-            collective_id=0, has_side_effects=True, vmem_limit_bytes=63 * 1024 * 1024
+            collective_id=0, has_side_effects=True, vmem_limit_bytes=538 * 1024 * 1024 // 10
         ),
     )(block_rows, block_cols, counts, block_tiles, start)
 

time: 123 us -> 120 us (0.976)
  Pallas kernels: 120 us -> 117 us
    pallas_call x1, Pallas kernels: 120 us -> 117 us  [shards(): pl.pallas_call(kernel, out_shape=(jax.ShapeDtypeStruct((64, 2 * HALF), BF...]
where the time goes in v4:
time: 120 us
  Pallas kernels  117 us (98%)
  local copies, waits for them, and re-layouts  1.89 us (2%)
  between operations  1.3 us (1%)
    pallas_call x1, Pallas kernels, shards(): pl.pallas_call(kernel, out_shape=(jax.ShapeDtypeStruct((64, 2 * HALF), BF...  117 us

profile of v4, /device:TPU:1, one launch (start us, length us, event | category | flops | bytes accessed | tf_op | source)
XLA Modules:
  0.0 120.2 jit_solution(12516041962916428822)
XLA Ops:
  1.3 0.0 copy-start
  1.3 0.0 copy-start.1
  1.3 0.6 copy-done
  1.9 0.0 copy-done.1
  1.9 117.1 %shard_map.68 = (bf16[64,256]{1,0:T(8,128)(2,1)S(1)}, bf16[64,256]{1,0:T(8,128)(2,1)S(1)}) custom-call(s32[1,20]{1,0:T(1,128)S(1)} %copy-done, s32[1,20]{1,0:T(1,128)S(1)} %copy-done.1, s32[1,1]{1,0:T(1,128)S(6)} %copy.9.counts_ref, bf16[1,20,128,128]{3,2,1,0:T(8,128)(2,1)} %tiles_ref.1, bf16[4,4,64,256]{3,2,1,0:T(8,128)(2,1)} %bitcast.1), custom_call_target="tpu_custom_call" | custom-call | tf_op jit(solution)/shard_map/pallas_call | solution.py:410
  119.0 0.6 copy.10
  119.6 0.6 copy.11
Async XLA Ops:
  1.3 0.7 copy-start
  1.3 0.7 copy-start.1

commit v5 on v4

--- a/solution.py
+++ b/solution.py
@@ -19,6 +19,11 @@
 
 TO_OWNER = (5, -5, 3, -3, 2, -2, 1, -1)
 RELAYED = (3, 2, 1, -1)
+
+FAR_FIRST = (
+    (10, 9, 11, 6, 14, 5, 7, 13, 15, 8, 2, 1, 3, 4, 12),
+    (8, 9, 7, 10, 6, 11, 5, 12, 4, 13, 3, 14, 2, 15, 1),
+)
 
 
 def kernel(
@@ -53,7 +58,7 @@
 
     def norm_dev(stage, k):
         if stage == 0:
-            return ((row + k) % 16, col)
+            return at(x + k // 4, y + k % 4, z, c)
         return (row, ((z + k) % 16) * 2 + c)
 
     barrier = pltpu.get_barrier_semaphore()
@@ -161,6 +166,8 @@
             return carry
 
         lax.fori_loop(0, 2, outer, 0)
+        if it == 0:
+            give_turn()
 
         def near(k, carry):
             m = 11 + 2 * k
@@ -256,24 +263,34 @@
         pending.append(functools.partial(xy_drain, it, 0, 1, s2.at[it, :, pl.ds(0, 3)]))
         return [total(1, h, s2, r2) for h in range(4)]
 
-    def piece_ref(it, h, stage, axis, g):
-        if stage == 0:
-            return bas.at[it, h, g, y] if axis == 0 else bas.at[it, h, x, g]
-        return bas.at[it, h, g] if axis == 0 else bas.at[it, h, :, g]
-
     def three(it, stage, h):
         return bas.at[it, h, 0, pl.ds(0, 3)] if stage == 0 else bas.at[it, h, pl.ds(0, 3)]
 
-    def xy_gather(it, stage, axes, late):
-        for k in (2, 1, 3):
+    def xy_gather(it, late):
+        def block(h, i, j):
+            return bas.at[it, h, j, i] if h == 0 else bas.at[it, h, i, j]
+
+        def send(stage, h, ref):
+            for k in (2, 1, 3):
+                xy_copy(it, 1, stage, h, k, 1 - (h + stage) % 2, ref, ref).start()
+
+        def arrived(stage, h):
+            part = three(it, stage, h)
+            xy_copy(it, 1, stage, h, 1, 0, part, part).wait_recv()
+
+        place = [(coord(1 - h), coord(h)) for h in (0, 1)]
+        for stage in (0, 1):
             for h in (0, 1):
-                ref = piece_ref(it, h, stage, axes[h], coord(axes[h]))
-                xy_copy(it, 1, stage, h, k, axes[h], ref, ref).start()
-        pending.append(functools.partial(xy_drain, it, 1, stage, three(it, stage, slice(None))))
+                send(stage, h, block(h, *place[h]))
         late()
         for h in (0, 1):
-            part = three(it, stage, h)
-            xy_copy(it, 1, stage, h, 1, 0, part, part).wait_recv()
+            arrived(0, h)
+            for k in (1, 2, 3):
+                send(1, h, block(h, (place[h][0] + k) % 4, place[h][1]))
+        for h in (0, 1):
+            arrived(1, h)
+        for stage in (0, 1):
+            pending.append(functools.partial(xy_drain, it, 1, stage, three(it, stage, slice(None))))
 
     def norm_copy(it, stage, src, dst, k):
         return remote(src, dst, ns.at[it, stage], nr.at[it, stage], norm_dev(stage, k))
@@ -281,11 +298,8 @@
     def norm_start(it, stage, value):
         nbuf[it, stage, 0] = jnp.broadcast_to(value, (8, HALF))
 
-        def one(k, carry):
+        for k in FAR_FIRST[stage]:
             norm_copy(it, stage, nbuf.at[it, stage, 0], nbuf.at[it, stage, k], k).start()
-            return carry
-
-        lax.fori_loop(1, 16, one, 0)
         rest = nbuf.at[it, stage, pl.ds(1, 15)]
         pending.append(norm_copy(it, stage, rest, rest, 1).wait_send)
 
@@ -314,8 +328,6 @@
                 norm_start(0, 1, norm_finish(0, 0))
 
         own = z_reduce(it, share_norm)
-        if it == 0:
-            give_turn()
         pending.append(functools.partial(z_drain, it, 0))
         if it == 1:
             own = own * scale_of(norm_finish(0, 1))
@@ -351,8 +363,7 @@
             low = rows.astype(BF16)
             bas[1, 0, x, y] = low[:64]
             bas[1, 1, x, y] = low[64:]
-            xy_gather(1, 0, (1, 0), functools.partial(norm_start, 0, 0, squares))
-            xy_gather(1, 1, (0, 1), lambda: None)
+            xy_gather(1, functools.partial(norm_start, 0, 0, squares))
         else:
             norm_start(1, 0, squares)
             zfin[...] = rows

time: 120 us -> 119 us (level)
  no operation moved by 1% of the time
where the time goes in v5:
time: 119 us
  Pallas kernels  116 us (97%)
  local copies, waits for them, and re-layouts  1.89 us (2%)
  between operations  1.3 us (1%)
    pallas_call x1, Pallas kernels, shards(): pl.pallas_call(kernel, out_shape=(jax.ShapeDtypeStruct((64, 2 * HALF), BF...  116 us

profile of v5, /device:TPU:1, one launch (start us, length us, event | category | flops | bytes accessed | tf_op | source)
XLA Modules:
  0.0 119.2 jit_solution(13754154764987312031)
XLA Ops:
  1.3 0.0 copy-start
  1.3 0.0 copy-start.1
  1.3 0.6 copy-done
  1.9 0.0 copy-done.1
  1.9 116.0 %shard_map.68 = (bf16[64,256]{1,0:T(8,128)(2,1)S(1)}, bf16[64,256]{1,0:T(8,128)(2,1)S(1)}) custom-call(s32[1,20]{1,0:T(1,128)S(1)} %copy-done, s32[1,20]{1,0:T(1,128)S(1)} %copy-done.1, s32[1,1]{1,0:T(1,128)S(6)} %copy.9.counts_ref, bf16[1,20,128,128]{3,2,1,0:T(8,128)(2,1)} %tiles_ref.1, bf16[4,4,64,256]{3,2,1,0:T(8,128)(2,1)} %bitcast.1), custom_call_target="tpu_custom_call" | custom-call | tf_op jit(solution)/shard_map/pallas_call | solution.py:421
  118.0 0.6 copy.10
  118.6 0.6 copy.11
Async XLA Ops:
  1.3 0.7 copy-start
  1.3 0.7 copy-start.1

commit v6 on v5

--- a/solution.py
+++ b/solution.py
@@ -66,16 +66,13 @@
     def greet(dev):
         pl.semaphore_signal(barrier, inc=1, device_id=dev, device_id_type=pl.DeviceIdType.MESH)
 
-    greet(partner)
-
-    def greet_line(k, carry):
+    for k in (3, 2, 1):
         greet(zdev(k))
         greet(zdev(-k))
+    for k in (2, 1, 3):
         greet(at(x + k, y, z, c))
         greet(at(x, y + k, z, c))
-        return carry
-
-    lax.fori_loop(1, 4, greet_line, 0)
+    greet(partner)
 
     local = [
         pltpu.make_async_copy(rows_ref, srows, loc_sem.at[0]),

time: 119 us -> 119 us (level)
  no operation moved by 1% of the time
where the time goes in v6:
time: 119 us
  Pallas kernels  116 us (97%)
  local copies, waits for them, and re-layouts  1.89 us (2%)
  between operations  1.3 us (1%)
    pallas_call x1, Pallas kernels, shards(): pl.pallas_call(kernel, out_shape=(jax.ShapeDtypeStruct((64, 2 * HALF), BF...  116 us

profile of v6, /device:TPU:1, one launch (start us, length us, event | category | flops | bytes accessed | tf_op | source)
XLA Modules:
  0.0 118.9 jit_solution(15585438724399978711)
XLA Ops:
  1.3 0.0 copy-start
  1.3 0.0 copy-start.1
  1.3 0.6 copy-done
  1.9 0.0 copy-done.1
  1.9 115.7 %shard_map.68 = (bf16[64,256]{1,0:T(8,128)(2,1)S(1)}, bf16[64,256]{1,0:T(8,128)(2,1)S(1)}) custom-call(s32[1,20]{1,0:T(1,128)S(1)} %copy-done, s32[1,20]{1,0:T(1,128)S(1)} %copy-done.1, s32[1,1]{1,0:T(1,128)S(6)} %copy.9.counts_ref, bf16[1,20,128,128]{3,2,1,0:T(8,128)(2,1)} %tiles_ref.1, bf16[4,4,64,256]{3,2,1,0:T(8,128)(2,1)} %bitcast.1), custom_call_target="tpu_custom_call" | custom-call | tf_op jit(solution)/shard_map/pallas_call | solution.py:418
  117.7 0.6 copy.10
  118.3 0.6 copy.11
Async XLA Ops:
  1.3 0.7 copy-start
  1.3 0.7 copy-start.1
